TPU v7x, 32 devices: a whole 2x2x4 slice. The times are simulated.
32 devices in a mesh: expert: 16 (over z, y, x), mp: 2 (over core).
Axes of the slice: x: 2, y: 2, z: 4, core: 2. Of those that a mesh axis runs over, the one named last changes fastest.
Arguments:
- partials: bfloat16 [16, 2, 1024, 768], P('expert', None, None, 'mp'), may hold values from -6 to 6
- counts: int32 [8], replicated, may hold values from 1 to 8, as said below
- slot_expert: int32 [16], replicated, may hold values from 0 to 7, as said below
- owner: int32 [16], replicated, may hold values from 0 to 15, each once
- left: float32 [16, 1024, 1024], P('expert', 'mp')
- right: float32 [16, 768, 768], P('expert', 'mp')
- left_root: bfloat16 [16, 1024, 1024], P('expert'), as said below
- right_root: bfloat16 [16, 768, 768], P('expert', 'mp'), as said below
Outputs:
- update: bfloat16 [16, 2, 1024, 768], P('expert', None, None, 'mp')
- left_next: float32 [16, 1024, 1024], P('expert', 'mp')
- right_next: float32 [16, 768, 768], P('expert', 'mp')
Inputs may be any that keep to these rules, and one draw needn't show every extreme that they name: counts[e] is the number of entries of slot_expert equal to e; they sum to 16 and one expert has exactly 8. `slot_expert`: every expert is named by some entry. `owner`: each device owns exactly one block. `left_root`: each matrix is symmetric. `right_root`: each matrix is symmetric.
All inputs are finite; a program needn't handle non-finite values.
Results may differ from a plain program's by a relative error of at most 0.0052.
Values may be sent and summed in bfloat16 or wider, within the bound.
A program may use at most 64 MiB of HBM per device.

v0:
```python
import jax
import jax.numpy as jnp
from jax import lax
from jax.sharding import PartitionSpec as P


def on_device(partials, counts, slot_expert, owner, left, right, left_root, right_root):
    devices = lax.axis_size("expert")
    halves = partials.shape[1]
    row_count = partials.shape[2]
    slab_rows = row_count // devices
    experts = counts.shape[0]
    counts_float = counts.astype(jnp.float32)
    labels = jnp.arange(experts, dtype=jnp.int32)
    onehot = (slot_expert[None, :] == labels[:, None]).astype(jnp.bfloat16)
    positions = jnp.arange(devices, dtype=jnp.int32)
    inverse = jnp.zeros((devices,), jnp.int32).at[owner].set(positions)
    own_slot = partials[0]
    spread = lax.all_to_all(own_slot, "expert", split_axis=1, concat_axis=0, tiled=True)
    col_width = spread.shape[2]
    flattened = spread.reshape(devices, halves * slab_rows * col_width)
    summed = jnp.dot(onehot, flattened, preferred_element_type=jnp.float32)
    averaged = (summed / counts_float[:, None]).astype(jnp.bfloat16)
    ordered = averaged.reshape(experts * halves, slab_rows, col_width)
    arrived = lax.all_to_all(
        jnp.take(ordered, inverse, axis=0), "expert", split_axis=0, concat_axis=0, tiled=True
    )
    grad_cols = arrived.reshape(row_count, arrived.shape[2])
    grad_full = lax.all_gather(grad_cols, "mp", axis=1, tiled=True)
    half_rows = left.shape[1]
    grad_rows = lax.dynamic_slice_in_dim(grad_full, lax.axis_index("mp") * half_rows, half_rows, 0)
    full_cols = grad_full.shape[1]
    left_next = (
        left[0]
        + lax.dot_general(
            grad_rows, grad_full, (((1,), (1,)), ((), ())), preferred_element_type=jnp.float32
        )
        / full_cols
    )
    right_next = (
        right[0]
        + lax.dot_general(
            grad_cols, grad_full, (((0,), (0,)), ((), ())), preferred_element_type=jnp.float32
        )
        / row_count
    )
    middle = lax.dot_general(
        grad_full, right_root[0], (((1,), (1,)), ((), ())), preferred_element_type=jnp.float32
    ).astype(jnp.bfloat16)
    precond = jnp.dot(left_root[0], middle, preferred_element_type=jnp.float32).astype(jnp.bfloat16)
    outgoing = precond.reshape(devices, slab_rows, precond.shape[1])
    middles = lax.all_to_all(outgoing, "expert", split_axis=0, concat_axis=0, tiled=True)
    col_width = middles.shape[2]
    by_block = jnp.take(middles, owner, axis=0).reshape(experts, halves * slab_rows * col_width)
    per_slot = jnp.take(by_block, slot_expert, axis=0)
    returned = lax.all_to_all(
        per_slot.reshape(devices, halves, slab_rows, col_width),
        "expert",
        split_axis=0,
        concat_axis=2,
        tiled=True,
    )
    return (returned, left_next[None], right_next[None])


def solution(mesh):
    return jax.shard_map(
        on_device,
        mesh=mesh,
        in_specs=(
            P("expert", None, None, "mp"),
            P(),
            P(),
            P(),
            P("expert", "mp", None),
            P("expert", "mp", None),
            P("expert", None, None),
            P("expert", "mp", None),
        ),
        out_specs=(P("expert", None, None, "mp"), P("expert", "mp", None), P("expert", "mp", None)),
        check_vma=False,
    )
```

profile of v0, /device:TPU:9, one launch (start us, length us, event | category | flops | bytes accessed | tf_op | source)
XLA Modules:
  0.0 186.5 jit_solution(11275313911782543089)
XLA Ops:
  7.2 0.0 copy-start
  7.2 4.3 %copy.23 = bf16[1,2,1024,384]{3,1,2,0:T(2,128)(2,1)} copy(bf16[1,2,1024,384]{3,2,1,0:T(8,128)(2,1)} %param.10) | data formatting | bytes 3145728 | tf_op args[0]
  11.5 6.8 %all-to-all-start = ((bf16[2,1024,384]{2,0,1:T(2,128)(2,1)}), bf16[2,1024,384]{2,0,1:T(2,128)(2,1)}, u32[]{:S(2)}, u32[]{:S(2)}) async-start(bf16[2,1024,384]{2,0,1:T(2,128)(2,1)} %bitcast.46), calls=%async_computation | async-start | bytes 3145728 | tf_op jit(solution)/shard_map/all_to_all | solution.py:19
  18.3 0.0 all-gather.2.cloned.1.call-start
  18.4 0.6 scatter_custom_fusion
  19.1 34.8 %all-to-all-done = bf16[2,1024,384]{2,0,1:T(2,128)(2,1)} async-done(((bf16[2,1024,384]{2,0,1:T(2,128)(2,1)}), bf16[2,1024,384]{2,0,1:T(2,128)(2,1)}, u32[]{:S(2)}, u32[]{:S(2)}) %all-to-all-start) | async-done | bytes 1572896 | tf_op jit(solution)/shard_map/all_to_all | solution.py:19
  53.9 1.7 copy.17
  55.6 0.0 copy-start.7
  55.6 0.9 copy.20
  56.5 0.3 fusion
  56.9 1.2 reshape.42
  58.1 1.8 gather_fusion.1
  60.0 0.2 broadcast_select_fusion.2
  60.2 0.0 copy-start.4
  60.2 24.9 %all_to_all.43 = bf16[16,64,384]{2,1,0:T(8,128)(2,1)} all-to-all(bf16[16,64,384]{2,1,0:T(8,128)(2,1)S(1)} %broadcast_select_fusion.2), channel_id=1, replica_groups=mesh['expert'=16,'mp'=2] {'expert'}, dimensions={0} | all-to-all | bytes 1572864 | tf_op jit(solution)/shard_map/all_to_all | solution.py:25
  85.1 0.0 all-gather.2.cloned.1.call-update
  85.1 10.4 %all-gather.2.cloned.1.call-done = bf16[1024,768]{1,0:T(8,128)(2,1)} async-done(((bf16[1024,384]{1,0:T(8,128)(2,1)}), bf16[1024,768]{1,0:T(8,128)(2,1)}) %all-gather.2.cloned.1.call-update) | async-done | bytes 1572880 | tf_op jit(solution)/shard_map/all_gather | solution.py:29
  95.5 3.2 %fusion.9 = bf16[1024,384]{0,1:T(8,128)(2,1)S(1)} fusion(bf16[1,1024,1024]{2,1,0:T(8,128)(2,1)S(1)} %copy-done, bf16[1024,768]{1,0:T(8,128)(2,1)} %all-gather.2.cloned.1.call-done, bf16[1,384,768]{2,1,0:T(8,128)(2,1)S(1)} %copy-done.4), kind=kOutput, calls=%fused_computation.17 | convolution fusion | flops 1410072576 | bytes 5046272 | tf_op jit(solution)/shard_map/dot_general | solution.py:50
  98.7 1.2 copy.18
  99.9 6.4 %all-to-all-start.2 = ((bf16[16,64,384]{2,1,0:T(8,128)(2,1)}), bf16[16,64,384]{2,1,0:T(8,128)(2,1)S(1)}, u32[]{:S(2)}, u32[]{:S(2)}) async-start(bf16[16,64,384]{2,1,0:T(8,128)(2,1)} %bitcast.52), calls=%async_computation.2 | async-start | bytes 1572864 | tf_op jit(solution)/shard_map/all_to_all | solution.py:52
  106.3 19.0 %all-to-all-done.2 = bf16[16,64,384]{2,1,0:T(8,128)(2,1)S(1)} async-done(((bf16[16,64,384]{2,1,0:T(8,128)(2,1)}), bf16[16,64,384]{2,1,0:T(8,128)(2,1)S(1)}, u32[]{:S(2)}, u32[]{:S(2)}) %all-to-all-start.2) | async-done | bytes 786464 | tf_op jit(solution)/shard_map/all_to_all | solution.py:52
  125.3 1.5 gather_fusion.2
  126.9 2.2 %broadcast_select_fusion.1 = bf16[16,64,384]{2,1,0:T(8,128)(2,1)} fusion(bf16[16,64,384]{2,1,0:T(8,128)(2,1)} %gather_fusion.2, pred[16]{0:T(512)(128)(4,1)S(1)} %compare_and_fusion), kind=kLoop, calls=%fused_computation.19 | loop fusion | flops 393216 | bytes 1572880 | tf_op jit(solution)/shard_map/jit(_take)/select_n | solution.py:54
  129.0 1.5 reshape.45
  130.5 2.7 %gather_fusion = bf16[16,49152]{1,0:T(8,128)(2,1)} fusion(bf16[8,49152]{1,0:T(8,128)(2,1)S(1)} %reshape.45, s32[1024]{0:T(1024)S(1)} %pad_clamp_fusion), kind=kCustom, calls=%fused_computation.2 | custom fusion | bytes 3145792 | tf_op jit(solution)/shard_map/jit(_take)/gather | solution.py:55
  133.3 1.7 copy.21
  134.9 1.4 broadcast_select_fusion
  136.3 4.8 %all-to-all-start.3 = ((bf16[16,2,64,384]{3,2,1,0:T(8,128)(2,1)}), bf16[16,2,64,384]{3,2,1,0:T(8,128)(2,1)}, u32[]{:S(2)}, u32[]{:S(2)}) async-start(bf16[16,2,64,384]{3,2,1,0:T(8,128)(2,1)} %broadcast_select_fusion), calls=%async_computation.3 | async-start | bytes 3145728 | tf_op jit(solution)/shard_map/all_to_all | solution.py:56
  141.1 3.7 %fusion.5 = f32[1,384,768]{2,1,0:T(8,128)} fusion(bf16[1024,384]{1,0:T(8,128)(2,1)S(1)} %bitcast.51, bf16[1024,768]{1,0:T(8,128)(2,1)} %all-gather.2.cloned.1.call-done, f32[1,384,768]{2,1,0:T(8,128)} %param.15), kind=kOutput, calls=%fused_computation.15 | convolution fusion | flops 604569600 | bytes 4718592 | tf_op jit(solution)/shard_map/dot_general | solution.py:42
  144.9 2.3 %fusion.1 = f32[1,512,1024]{2,1,0:T(8,128)} fusion(f32[1,512,1024]{2,1,0:T(8,128)S(1)} %copy-done.2, bf16[1024,768]{1,0:T(8,128)(2,1)S(1)} %copy-done.3, s32[]{:T(128)S(6)} %select_n.25), kind=kOutput, calls=%fused_computation.7 | convolution fusion | flops 806354944 | bytes 6553604 | tf_op jit(solution)/shard_map/dot_general | solution.py:35
  147.2 29.7 %all-to-all-done.3 = bf16[16,2,64,384]{3,2,1,0:T(8,128)(2,1)} async-done(((bf16[16,2,64,384]{3,2,1,0:T(8,128)(2,1)}), bf16[16,2,64,384]{3,2,1,0:T(8,128)(2,1)}, u32[]{:S(2)}, u32[]{:S(2)}) %all-to-all-start.3) | async-done | bytes 1572896 | tf_op jit(solution)/shard_map/all_to_all | solution.py:56
  176.9 2.7 %copy.19 = bf16[1,2,16,64,384]{4,3,2,1,0:T(8,128)(2,1)} copy(bf16[1,2,16,64,384]{4,3,1,2,0:T(8,128)(2,1)} %bitcast.9) | data formatting | bytes 3145728 | tf_op jit(solution)/shard_map/all_to_all | solution.py:56
  (24 shorter events, 0.1 us)
Async XLA Ops:
  7.2 88.3 %copy-start = (bf16[1,1024,1024]{2,1,0:T(8,128)(2,1)S(1)}, bf16[1,1024,1024]{2,1,0:T(8,128)(2,1)}, u32[]{:S(2)}) copy-start(bf16[1,1024,1024]{2,1,0:T(8,128)(2,1)} %param.16) | copy-start | bytes 6291460
  11.5 6.8 %copy-start.5 = (s32[8]{0:T(128)S(1)}, s32[8]{0:T(128)}, u32[]{:S(2)}) copy-start(s32[8]{0:T(128)} %param.11) | copy-start | bytes 100
  11.5 6.9 %copy-start.6 = (s32[16]{0:T(128)S(1)}, s32[16]{0:T(128)}, u32[]{:S(2)}) copy-start(s32[16]{0:T(128)} %param.13) | copy-start | bytes 196
  11.5 42.4 %all-to-all-start = ((bf16[2,1024,384]{2,0,1:T(2,128)(2,1)}), bf16[2,1024,384]{2,0,1:T(2,128)(2,1)}, u32[]{:S(2)}, u32[]{:S(2)}) async-start(bf16[2,1024,384]{2,0,1:T(2,128)(2,1)} %bitcast.46), calls=%async_computation | async-start | bytes 3145728 | tf_op jit(solution)/shard_map/all_to_all | solution.py:19
  18.3 77.2 %all-gather.2.cloned.1.call-start = ((), (), s32[]{:S(2)}) async-start(), calls=%async_computation.4 | async-start | bytes 2359296 | tf_op jit(solution)/shard_map/all_gather | solution.py:29
  55.6 0.9 copy-start.7
  60.2 35.3 %copy-start.4 = (bf16[1,384,768]{2,1,0:T(8,128)(2,1)S(1)}, bf16[1,384,768]{2,1,0:T(8,128)(2,1)}, u32[]{:S(2)}) copy-start(bf16[1,384,768]{2,1,0:T(8,128)(2,1)} %param.17) | copy-start | bytes 1769476
  99.9 25.5 %all-to-all-start.2 = ((bf16[16,64,384]{2,1,0:T(8,128)(2,1)}), bf16[16,64,384]{2,1,0:T(8,128)(2,1)S(1)}, u32[]{:S(2)}, u32[]{:S(2)}) async-start(bf16[16,64,384]{2,1,0:T(8,128)(2,1)} %bitcast.52), calls=%async_computation.2 | async-start | bytes 1572864 | tf_op jit(solution)/shard_map/all_to_all | solution.py:52
  136.3 4.8 %copy-start.1 = (bf16[16,64,384]{2,1,0:T(8,128)(2,1)S(1)}, bf16[16,64,384]{2,1,0:T(8,128)(2,1)}, u32[]{:S(2)}) copy-start(bf16[16,64,384]{2,1,0:T(8,128)(2,1)} %all_to_all.43) | copy-start | bytes 2359300
  136.3 40.6 %all-to-all-start.3 = ((bf16[16,2,64,384]{3,2,1,0:T(8,128)(2,1)}), bf16[16,2,64,384]{3,2,1,0:T(8,128)(2,1)}, u32[]{:S(2)}, u32[]{:S(2)}) async-start(bf16[16,2,64,384]{3,2,1,0:T(8,128)(2,1)} %broadcast_select_fusion), calls=%async_computation.3 | async-start | bytes 3145728 | tf_op jit(solution)/shard_map/all_to_all | solution.py:56
  141.1 3.7 %copy-start.2 = (f32[1,512,1024]{2,1,0:T(8,128)S(1)}, f32[1,512,1024]{2,1,0:T(8,128)}, u32[]{:S(2)}) copy-start(f32[1,512,1024]{2,1,0:T(8,128)} %param.14) | copy-start | bytes 6291460
  141.1 3.7 %copy-start.3 = (bf16[1024,768]{1,0:T(8,128)(2,1)S(1)}, bf16[1024,768]{1,0:T(8,128)(2,1)}, u32[]{:S(2)}) copy-start(bf16[1024,768]{1,0:T(8,128)(2,1)} %all-gather.2.cloned.1.call-done) | copy-start | bytes 4718596
Sparse Core Ops, SparseCore 0:
  85.2 10.2 all-gather.1
where the time goes:
time: 189 us; the launch traced here: 186 us
  waiting for transfers between devices  93.9 us (50%)
  blocking collectives  24.9 us (13%)
  local copies, waits for them, and re-layouts  22 us (12%)
  starting transfers between devices  18 us (10%)
  between operations  14.2 us (8%)
  matrix products  9.62 us (5%)
  other arithmetic  3.78 us (2%)
    all_to_all x1, waiting for transfers between devices, on_device(): lax.all_to_all(own_slot, 'expert', split_axis=1, concat_axis=0, tiled=True)  34.8 us
    all_to_all x1, waiting for transfers between devices, on_device(): lax.all_to_all(per_slot.reshape(devices, halves, slab_rows, col_width), '...  29.7 us
    all_to_all x1, blocking collectives, on_device(): lax.all_to_all(jnp.take(ordered, inverse, axis=0), 'expert', split_axis=0...  24.9 us
    all_to_all x1, waiting for transfers between devices, on_device(): lax.all_to_all(outgoing, 'expert', split_axis=0, concat_axis=0, tiled=True)  19 us
    all_gather x1, waiting for transfers between devices, on_device(): grad_full = lax.all_gather(grad_cols, 'mp', axis=1, tiled=True)  10.4 us
    unnamed x19, local copies, waits for them, and re-layouts  6.95 us
    all_to_all x1, starting transfers between devices, on_device(): lax.all_to_all(own_slot, 'expert', split_axis=1, concat_axis=0, tiled=True)  6.8 us
    all_to_all x1, starting transfers between devices, on_device(): lax.all_to_all(outgoing, 'expert', split_axis=0, concat_axis=0, tiled=True)  6.41 us
  transfers between devices with their start and end apart: 4, of which 4 were waited for; matrix products, arithmetic and copies ran while one was open for 4% of the time, Pallas kernels for 0%

commit v1 on v0

v1 whole, which is shorter than its diff:
```python
import functools

import jax
import jax.numpy as jnp
from jax import lax
from jax.experimental import pallas as pl
from jax.experimental.pallas import tpu as pltpu
from jax.sharding import PartitionSpec as P

GROUPS = 2
CHUNKS = 4
AHEAD = 2


def kernel(
    n, groups, chunks, table, partials, left, right, left_root, right_root,
    update, left_next, right_next,
    arrived, running, sums, blocks, grad, middle, precond, spread, picked,
    left_buf, right_buf, lroot_buf, rroot_buf,
    load_sem, send_a, recv_a, send_b, recv_b, send_p, recv_p, send_c, recv_c, send_d, recv_d, store_sem,
):
    size = n // groups
    halves, rows, cols = partials.shape[1:]
    part = rows // chunks
    sub = part // size
    full_cols = grad.shape[1]
    me = lax.axis_index("expert")
    core = lax.axis_index("mp")
    first = me // size * size
    place = lax.rem(me, size)
    keep_at, source_at, half_at = size, 2 * size, 2 * size + n
    fetch_at, count_at = 2 * size + 2 * n, 2 * size + 2 * n + halves * size

    def remote(src, dst, send, recv, peer):
        return pltpu.make_async_remote_copy(
            src_ref=src, dst_ref=dst, send_sem=send, recv_sem=recv,
            device_id=peer, device_id_type=pl.DeviceIdType.MESH,
        )

    def wait_bytes(ref, sem):
        pltpu.make_async_copy(ref, ref, sem).wait()

    def row_slab(chunk, index):
        return pl.ds(pl.multiple_of(chunk * part + index * sub, sub), sub)

    my_cols = pl.ds(pl.multiple_of(core * cols, 128), cols)

    loads = [
        pltpu.make_async_copy(right_root.at[0], rroot_buf, load_sem.at[0]),
        pltpu.make_async_copy(left_root.at[0], lroot_buf, load_sem.at[1]),
        pltpu.make_async_copy(left.at[0], left_buf, load_sem.at[2]),
        pltpu.make_async_copy(right.at[0], right_buf, load_sem.at[3]),
    ]

    barrier = pltpu.get_barrier_semaphore()

    def greet(step, carry):
        pl.semaphore_signal(
            barrier, inc=1, device_id={"expert": lax.rem(me + step, n)},
            device_id_type=pl.DeviceIdType.MESH,
        )
        return carry

    lax.fori_loop(1, n, greet, 0)
    pl.semaphore_signal(barrier, inc=1, device_id={"mp": 1 - core}, device_id_type=pl.DeviceIdType.MESH)
    pl.semaphore_wait(barrier, n)

    def scatter_partials(chunk):
        def body(step, carry):
            index = lax.rem(place + step, size)
            remote(
                partials.at[0, :, row_slab(chunk, index), :],
                arrived[chunk].at[place], send_a.at[chunk], recv_a.at[chunk],
                {"expert": first + index},
            ).start()
            return carry

        lax.fori_loop(1, size, body, 0)
        pltpu.make_async_copy(
            partials.at[0, :, row_slab(chunk, place), :], arrived[chunk].at[place], recv_a.at[chunk]
        ).start()

    def send_sums(chunk):
        wait_bytes(arrived[chunk], recv_a.at[chunk])
        for half in range(halves):
            def add(rank, total):
                keep = table[keep_at + rank].astype(jnp.float32)
                total = total * keep + arrived[chunk][table[rank], half].astype(jnp.float32)
                running[rank, half] = total.astype(jnp.bfloat16)
                return total

            lax.fori_loop(0, size, add, jnp.zeros((sub, cols), jnp.float32))

        def send(step, carry):
            peer = lax.rem(me + step, n)
            sums[chunk, peer] = running[table[source_at + peer], table[half_at + peer]]
            remote(
                sums.at[chunk, peer], blocks.at[chunk, me], send_b.at[chunk], recv_b.at[chunk],
                {"expert": peer},
            ).start()
            return carry

        lax.fori_loop(1, n, send, 0)
        sums[chunk, me] = running[table[source_at + me], table[half_at + me]]
        pltpu.make_async_copy(sums.at[chunk, me], blocks.at[chunk, me], recv_b.at[chunk]).start()

    def form_grad(chunk):
        wait_bytes(blocks.at[chunk], recv_b.at[chunk])
        count = table[count_at].astype(jnp.float32)

        def form(index, carry):
            total = blocks[chunk, index].astype(jnp.float32)
            for group in range(1, groups):
                total = total + blocks[chunk, group * size + index].astype(jnp.float32)
            grad[row_slab(chunk, index), my_cols] = (total / count).astype(jnp.bfloat16)
            return carry

        lax.fori_loop(0, size, form, 0)
        swap(chunk).start()

    def swap(chunk):
        rows_of = pl.ds(chunk * part, part)
        return remote(
            grad.at[rows_of, my_cols], grad.at[rows_of, my_cols],
            send_p.at[chunk], recv_p.at[chunk], {"mp": 1 - core},
        )

    def form_middle(chunk):
        rows_of = pl.ds(chunk * part, part)
        swap(chunk).wait_recv()
        middle[rows_of, :] = lax.dot_general(
            grad[rows_of, :], rroot_buf[...], (((1,), (1,)), ((), ())), preferred_element_type=jnp.float32
        ).astype(jnp.bfloat16)

    def scatter_precond(chunk):
        rows_of = pl.ds(chunk * part, part)
        precond[rows_of, :] = jnp.dot(
            lroot_buf[rows_of, :], middle[...], preferred_element_type=jnp.float32
        ).astype(jnp.bfloat16)

        def body(step, carry):
            peer = lax.rem(me + step, n)
            remote(
                precond.at[row_slab(chunk, lax.rem(peer, size)), :], spread[chunk].at[me],
                send_c.at[chunk], recv_c.at[chunk], {"expert": peer},
            ).start()
            return carry

        lax.fori_loop(1, n, body, 0)
        pltpu.make_async_copy(
            precond.at[row_slab(chunk, place), :], spread[chunk].at[me], recv_c.at[chunk]
        ).start()

    def return_blocks(chunk):
        wait_bytes(spread[chunk], recv_c.at[chunk])

        def pick(index):
            for half in range(halves):
                picked[chunk, index, half] = spread[chunk][table[fetch_at + halves * index + half]]

        def body(step, carry):
            index = lax.rem(place + step, size)
            pick(index)
            remote(
                picked.at[chunk, index], update.at[0, :, row_slab(chunk, place), :],
                send_d.at[chunk], recv_d.at[chunk], {"expert": first + index},
            ).start()
            return carry

        lax.fori_loop(1, size, body, 0)
        pick(place)
        pltpu.make_async_copy(
            picked.at[chunk, place], update.at[0, :, row_slab(chunk, place), :], recv_d.at[chunk]
        ).start()

    for chunk in range(min(AHEAD, chunks)):
        scatter_partials(chunk)
    for load in loads:
        load.start()
    running[size] = jnp.zeros_like(running[size])
    loads[0].wait()
    for chunk in range(chunks):
        send_sums(chunk)
        if chunk + AHEAD < chunks:
            scatter_partials(chunk + AHEAD)
    for chunk in range(chunks):
        form_grad(chunk)
        if chunk:
            form_middle(chunk - 1)
    form_middle(chunks - 1)
    loads[1].wait()
    for chunk in range(chunks):
        scatter_precond(chunk)

    half_rows = left_buf.shape[0]
    loads[2].wait()
    tile = 128

    def add_left(index, carry):
        rows_of = pl.ds(pl.multiple_of(index * tile, tile), tile)
        product = lax.dot_general(
            grad[pl.ds(pl.multiple_of(core * half_rows + index * tile, tile), tile), :], grad[...],
            (((1,), (1,)), ((), ())), preferred_element_type=jnp.float32,
        )
        left_buf[rows_of, :] = left_buf[rows_of, :] + product / full_cols
        return carry

    lax.fori_loop(0, half_rows // tile, add_left, 0)
    left_store = pltpu.make_async_copy(left_buf, left_next.at[0], store_sem.at[0])
    left_store.start()
    loads[3].wait()

    def add_right(index, carry):
        rows_of = pl.ds(pl.multiple_of(index * tile, tile), tile)
        product = lax.dot_general(
            grad[:, pl.ds(pl.multiple_of(core * cols + index * tile, tile), tile)], grad[...],
            (((0,), (0,)), ((), ())), preferred_element_type=jnp.float32,
        )
        right_buf[rows_of, :] = right_buf[rows_of, :] + product / rows
        return carry

    lax.fori_loop(0, cols // tile, add_right, 0)
    right_store = pltpu.make_async_copy(right_buf, right_next.at[0], store_sem.at[1])
    right_store.start()

    for chunk in range(chunks):
        return_blocks(chunk)
    left_store.wait()
    right_store.wait()
    for chunk in range(chunks):
        wait_bytes(arrived[chunk].at[pl.ds(0, size - 1)], send_a.at[chunk])
        wait_bytes(sums.at[chunk, pl.ds(0, n - 1)], send_b.at[chunk])
        swap(chunk).wait_send()
        wait_bytes(spread[chunk].at[pl.ds(0, n - 1)], send_c.at[chunk])
        wait_bytes(picked.at[chunk, pl.ds(0, size - 1)], send_d.at[chunk])
    for chunk in range(chunks):
        wait_bytes(update.at[0, :, pl.ds(chunk * part, part), :], recv_d.at[chunk])


def index_table(n, groups, halves, counts, slot_expert, owner):
    size = n // groups
    me = lax.axis_index("expert")
    experts = lax.dynamic_slice_in_dim(slot_expert, me // size * size, size)
    position = jnp.arange(size, dtype=jnp.int32)
    before = (experts[None, :] < experts[:, None]) | (
        (experts[None, :] == experts[:, None]) & (position[None, :] < position[:, None])
    )
    rank = jnp.sum(before, axis=1, dtype=jnp.int32)
    placed = rank[None, :] == position[:, None]
    order = jnp.sum(jnp.where(placed, position[None, :], 0), axis=1, dtype=jnp.int32)
    sorted_experts = jnp.sum(jnp.where(placed, experts[None, :], 0), axis=1, dtype=jnp.int32)
    previous = jnp.concatenate([jnp.full((1,), -1, jnp.int32), sorted_experts[:-1]])
    keep = (sorted_experts == previous).astype(jnp.int32)
    blocks = jnp.arange(n, dtype=jnp.int32)
    block_of = jnp.sum(jnp.where(owner[None, :] == blocks[:, None], blocks[None, :], 0), axis=1, dtype=jnp.int32)
    expert_of = block_of // halves
    same = experts[None, :] == expert_of[:, None]
    upto = jnp.sum(experts[None, :] <= expert_of[:, None], axis=1, dtype=jnp.int32)
    source = jnp.where(jnp.any(same, axis=1), upto - 1, size)
    wanted = (halves * experts[:, None] + jnp.arange(halves, dtype=jnp.int32)[None, :]).reshape(-1)
    fetch = jnp.sum(jnp.where(wanted[:, None] == blocks[None, :], owner[None, :], 0), axis=1, dtype=jnp.int32)
    mine = jnp.sum(jnp.where(blocks == me, expert_of, 0), dtype=jnp.int32)
    labels = jnp.arange(counts.shape[0], dtype=jnp.int32)
    count = jnp.sum(jnp.where(labels == mine, counts, 0), dtype=jnp.int32)
    return jnp.concatenate([order, keep, source, block_of % halves, fetch, count[None]])


def on_device(n, partials, counts, slot_expert, owner, left, right, left_root, right_root):
    halves, rows, cols = partials.shape[1:]
    groups = GROUPS
    size = n // groups
    chunks = max(1, min(CHUNKS, rows // (16 * size)))
    sub = rows // chunks // size
    full_cols = right.shape[2]
    table = index_table(n, groups, halves, counts, slot_expert, owner)
    anywhere = pl.BlockSpec(memory_space=pl.ANY)
    bf16 = jnp.bfloat16
    dma = pltpu.SemaphoreType.DMA
    update, left_next, right_next = pl.pallas_call(
        functools.partial(kernel, n, groups, chunks),
        out_shape=(
            jax.ShapeDtypeStruct(partials.shape, bf16),
            jax.ShapeDtypeStruct(left.shape, jnp.float32),
            jax.ShapeDtypeStruct(right.shape, jnp.float32),
        ),
        in_specs=[pl.BlockSpec(memory_space=pltpu.SMEM)] + [anywhere] * 5,
        out_specs=(anywhere,) * 3,
        scratch_shapes=[
            [pltpu.VMEM((size, halves, sub, cols), bf16)] * chunks,
            pltpu.VMEM((size + 1, halves, sub, cols), bf16),
            pltpu.VMEM((chunks, n, sub, cols), bf16),
            pltpu.VMEM((chunks, n, sub, cols), bf16),
            pltpu.VMEM((rows, full_cols), bf16),
            pltpu.VMEM((rows, cols), bf16),
            pltpu.VMEM((rows, cols), bf16),
            [pltpu.VMEM((n, sub, cols), bf16)] * chunks,
            pltpu.VMEM((chunks, size, halves, sub, cols), bf16),
            pltpu.VMEM(left.shape[1:], jnp.float32),
            pltpu.VMEM(right.shape[1:], jnp.float32),
            pltpu.VMEM(left_root.shape[1:], bf16),
            pltpu.VMEM(right_root.shape[1:], bf16),
            dma((4,)),
        ]
        + [dma((chunks,))] * 10
        + [dma((2,))],
        compiler_params=pltpu.CompilerParams(
            collective_id=0, has_side_effects=True, vmem_limit_bytes=48 * 1024 * 1024
        ),
    )(table, partials, left, right, left_root, right_root)
    return update, left_next, right_next


def solution(mesh):
    return jax.shard_map(
        functools.partial(on_device, mesh.shape["expert"]),
        mesh=mesh,
        in_specs=(
            P("expert", None, None, "mp"),
            P(),
            P(),
            P(),
            P("expert", "mp", None),
            P("expert", "mp", None),
            P("expert", None, None),
            P("expert", "mp", None),
        ),
        out_specs=(P("expert", None, None, "mp"), P("expert", "mp", None), P("expert", "mp", None)),
        check_vma=False,
    )
```

time: 189 us -> 114 us (0.60)
  Pallas kernels: 0 us -> 98.8 us
  waiting for transfers between devices: 93.9 us -> 0 us
  blocking collectives: 24.9 us -> 0 us
  starting transfers between devices: 18 us -> 0 us
  between operations: 14.2 us -> 0.68 us
  local copies, waits for them, and re-layouts: 22 us -> 9.03 us
  matrix products: 9.62 us -> 0 us
    pallas_call x0 -> x1, Pallas kernels: none -> 98.8 us  [on_device(): pl.pallas_call(functools.partial(kernel, n, groups, chunks), out_shape=(j...]
    all_to_all x3 -> x0, waiting for transfers between devices: 83.5 us -> none  [the longest x1 34.8 us: on_device(): lax.all_to_all(own_slot, 'expert', split_axis=1, concat_axis=0, tiled=True)]
    all_to_all x1 -> x0, blocking collectives: 24.9 us -> none  [on_device(): lax.all_to_all(jnp.take(ordered, inverse, axis=0), 'expert', split_axis=0...]
    all_to_all x3 -> x0, starting transfers between devices: 18 us -> none  [the longest x1 6.8 us: on_device(): lax.all_to_all(own_slot, 'expert', split_axis=1, concat_axis=0, tiled=True)]
    all_gather x1 -> x0, waiting for transfers between devices: 10.4 us -> none  [on_device(): grad_full = lax.all_gather(grad_cols, 'mp', axis=1, tiled=True)]
    dot_general x4 -> x0, matrix products: 9.62 us -> none  [the longest x1 3.72 us: on_device(): lax.dot_general(grad_cols, grad_full, (((0,), (0,)), ((), ())), preferred...]
    gather x3 -> x0, local copies, waits for them, and re-layouts: 6.11 us -> none  [the longest x1 2.73 us: on_device(): per_slot = jnp.take(by_block, slot_expert, axis=0)]
    all_to_all x2 -> x0, local copies, waits for them, and re-layouts: 4.45 us -> none  [the longest x1 2.73 us: on_device(): lax.all_to_all(per_slot.reshape(devices, halves, slab_rows, col_width), '...]
  transfers between devices with their start and end apart: 4 -> 0, of which waited for: 4 -> 0; matrix products, arithmetic and copies ran while one was open for 4% -> 0% of each run, Pallas kernels for 0% -> 0%
where the time goes in v1:
time: 114 us; the launch traced here: 113 us
  Pallas kernels  98.8 us (87%)
  local copies, waits for them, and re-layouts  9.03 us (8%)
  other arithmetic  4.82 us (4%)
    pallas_call x1, Pallas kernels, on_device(): pl.pallas_call(functools.partial(kernel, n, groups, chunks), out_shape=(j...  98.8 us
    unnamed x11, local copies, waits for them, and re-layouts  8.22 us

profile of v1, /device:TPU:9, one launch (start us, length us, event | category | flops | bytes accessed | tf_op | source)
XLA Modules:
  0.0 113.3 jit_solution(6560530870958167700)
XLA Ops:
  0.7 0.7 broadcast_multiply_fusion
  1.4 0.2 convert_reduce_fusion.1
  1.6 0.1 select_reduce_fusion.2
  1.7 0.1 compare_convert_fusion
  1.8 0.1 iota_add_fusion
  1.9 0.1 add.41
  1.9 0.8 select_reduce_fusion
  2.8 0.6 fusion.2
  3.4 1.9 %fusion.3 = s32[]{:T(128)} fusion(s32[8]{0:T(128)} %param.9, s32[]{:T(128)} %get-tuple-element.7), kind=kLoop, calls=%fused_computation.23 | loop fusion | flops 23 | bytes 40 | tf_op jit(solution)/shard_map/reduce_sum | solution.py:264
  5.4 0.1 convert_reduce_fusion
  5.5 0.1 compare_reduce_fusion
  5.6 0.7 concatenate.7.table
  6.3 0.0 copy-start
  6.3 1.4 %copy-done = bf16[1,2,1024,384]{3,2,1,0:T(8,128)(2,1)S(1)} copy-done((bf16[1,2,1024,384]{3,2,1,0:T(8,128)(2,1)S(1)}, bf16[1,2,1024,384]{3,2,1,0:T(8,128)(2,1)}, u32[]{:S(2)}) %copy-start) | copy-done | bytes 1572888
  7.7 0.0 copy-start.1
  7.7 1.3 %copy-done.1 = f32[1,384,768]{2,1,0:T(8,128)S(1)} copy-done((f32[1,384,768]{2,1,0:T(8,128)S(1)}, f32[1,384,768]{2,1,0:T(8,128)}, u32[]{:S(2)}) %copy-start.1) | copy-done | bytes 1179672
  9.0 0.0 copy-start.2
  9.0 1.1 copy-done.2
  10.0 98.8 %shard_map.103 = (bf16[1,2,1024,384]{3,2,1,0:T(8,128)(2,1)S(1)}, f32[1,512,1024]{2,1,0:T(8,128)}, f32[1,384,768]{2,1,0:T(8,128)S(1)}) custom-call(s32[65]{0:T(128)S(1)} %concatenate.7.table, bf16[1,2,1024,384]{3,2,1,0:T(8,128)(2,1)S(1)} %copy-done, f32[1,512,1024]{2,1,0:T(8,128)} %left.1, f32[1,384,768]{2,1,0:T(8,128)S(1)} %copy-done.1, ...), custom_call_target="tpu_custom_call" | custom-call | tf_op jit(solution)/shard_map/pallas_call | solution.py:279
  108.8 0.0 copy-start.3
  108.9 1.1 %copy.14 = bf16[1,2,1024,384]{3,2,1,0:T(8,128)(2,1)} copy(bf16[1,2,1024,384]{3,2,1,0:T(8,128)(2,1)S(1)} %get-tuple-element.15) | data formatting | bytes 3145728
  110.0 1.0 copy-done.3
  111.0 1.3 %copy.15 = f32[1,512,1024]{2,1,0:T(8,128)} copy(f32[1,512,1024]{2,1,0:T(8,128)S(1)} %copy-done.3) | data formatting | bytes 4194304
  112.3 1.0 copy.16
  (1 shorter events, 0.0 us)
Async XLA Ops:
  6.3 1.4 %copy-start = (bf16[1,2,1024,384]{3,2,1,0:T(8,128)(2,1)S(1)}, bf16[1,2,1024,384]{3,2,1,0:T(8,128)(2,1)}, u32[]{:S(2)}) copy-start(bf16[1,2,1024,384]{3,2,1,0:T(8,128)(2,1)} %partials.1) | copy-start | bytes 4718596
  7.7 1.3 %copy-start.1 = (f32[1,384,768]{2,1,0:T(8,128)S(1)}, f32[1,384,768]{2,1,0:T(8,128)}, u32[]{:S(2)}) copy-start(f32[1,384,768]{2,1,0:T(8,128)} %right.1) | copy-start | bytes 3538948
  9.0 1.1 copy-start.2
  108.8 2.2 %copy-start.3 = (f32[1,512,1024]{2,1,0:T(8,128)S(1)}, f32[1,512,1024]{2,1,0:T(8,128)}, u32[]{:S(2)}) copy-start(f32[1,512,1024]{2,1,0:T(8,128)} %get-tuple-element.16) | copy-start | bytes 6291460

commit v2 on v1

--- a/solution.py
+++ b/solution.py
@@ -9,13 +9,13 @@
 
 GROUPS = 2
 CHUNKS = 4
-AHEAD = 2
+AHEAD = 3
 
 
 def kernel(
-    n, groups, chunks, table, partials, left, right, left_root, right_root,
+    n, groups, chunks, counts, slot_expert, owner, partials, left, right, left_root, right_root,
     update, left_next, right_next,
-    arrived, running, sums, blocks, grad, middle, precond, spread, picked,
+    table, arrived, running, sums, blocks, grad, middle, precond, spread, picked,
     left_buf, right_buf, lroot_buf, rroot_buf,
     load_sem, send_a, recv_a, send_b, recv_b, send_p, recv_p, send_c, recv_c, send_d, recv_d, store_sem,
 ):
@@ -28,8 +28,7 @@
     core = lax.axis_index("mp")
     first = me // size * size
     place = lax.rem(me, size)
-    keep_at, source_at, half_at = size, 2 * size, 2 * size + n
-    fetch_at, count_at = 2 * size + 2 * n, 2 * size + 2 * n + halves * size
+    source_at, half_at = size, size + n
 
     def remote(src, dst, send, recv, peer):
         return pltpu.make_async_remote_copy(
@@ -80,20 +79,53 @@
             partials.at[0, :, row_slab(chunk, place), :], arrived[chunk].at[place], recv_a.at[chunk]
         ).start()
 
+    def block_at(device):
+        return lax.fori_loop(
+            0, n, lambda block, found: jnp.where(owner[block] == device, block, found), jnp.int32(0), unroll=8
+        )
+
+    def fill_table():
+        def link(index, carry):
+            expert = slot_expert[first + index]
+            table[index] = lax.fori_loop(
+                0, size,
+                lambda other, found: jnp.where(
+                    (slot_expert[first + other] == expert) & (other < index), other, found
+                ),
+                jnp.int32(size), unroll=8,
+            )
+            return carry
+
+        lax.fori_loop(0, size, link, 0)
+
+        def locate(device, carry):
+            block = block_at(device)
+            expert = block // halves
+            table[source_at + device] = lax.fori_loop(
+                0, size,
+                lambda other, found: jnp.where(slot_expert[first + other] == expert, other, found),
+                jnp.int32(size), unroll=8,
+            )
+            table[half_at + device] = block - expert * halves
+            return carry
+
+        lax.fori_loop(0, n, locate, 0)
+
+    def half_sum(device):
+        return running[table[source_at + device], table[half_at + device]].astype(jnp.bfloat16)
+
     def send_sums(chunk):
         wait_bytes(arrived[chunk], recv_a.at[chunk])
         for half in range(halves):
-            def add(rank, total):
-                keep = table[keep_at + rank].astype(jnp.float32)
-                total = total * keep + arrived[chunk][table[rank], half].astype(jnp.float32)
-                running[rank, half] = total.astype(jnp.bfloat16)
-                return total
-
-            lax.fori_loop(0, size, add, jnp.zeros((sub, cols), jnp.float32))
+            def add(index, carry):
+                running[index, half] = running[table[index], half] + arrived[chunk][index, half].astype(jnp.float32)
+                return carry
+
+            lax.fori_loop(0, size, add, 0)
 
         def send(step, carry):
             peer = lax.rem(me + step, n)
-            sums[chunk, peer] = running[table[source_at + peer], table[half_at + peer]]
+            sums[chunk, peer] = half_sum(peer)
             remote(
                 sums.at[chunk, peer], blocks.at[chunk, me], send_b.at[chunk], recv_b.at[chunk],
                 {"expert": peer},
@@ -101,12 +133,12 @@
             return carry
 
         lax.fori_loop(1, n, send, 0)
-        sums[chunk, me] = running[table[source_at + me], table[half_at + me]]
+        sums[chunk, me] = half_sum(me)
         pltpu.make_async_copy(sums.at[chunk, me], blocks.at[chunk, me], recv_b.at[chunk]).start()
 
     def form_grad(chunk):
         wait_bytes(blocks.at[chunk], recv_b.at[chunk])
-        count = table[count_at].astype(jnp.float32)
+        count = counts[block_at(me) // halves].astype(jnp.float32)
 
         def form(index, carry):
             total = blocks[chunk, index].astype(jnp.float32)
@@ -156,7 +188,7 @@
 
         def pick(index):
             for half in range(halves):
-                picked[chunk, index, half] = spread[chunk][table[fetch_at + halves * index + half]]
+                picked[chunk, index, half] = spread[chunk][owner[halves * slot_expert[first + index] + half]]
 
         def body(step, carry):
             index = lax.rem(place + step, size)
@@ -178,6 +210,7 @@
     for load in loads:
         load.start()
     running[size] = jnp.zeros_like(running[size])
+    fill_table()
     loads[0].wait()
     for chunk in range(chunks):
         send_sums(chunk)
@@ -235,34 +268,6 @@
         wait_bytes(picked.at[chunk, pl.ds(0, size - 1)], send_d.at[chunk])
     for chunk in range(chunks):
         wait_bytes(update.at[0, :, pl.ds(chunk * part, part), :], recv_d.at[chunk])
-
-
-def index_table(n, groups, halves, counts, slot_expert, owner):
-    size = n // groups
-    me = lax.axis_index("expert")
-    experts = lax.dynamic_slice_in_dim(slot_expert, me // size * size, size)
-    position = jnp.arange(size, dtype=jnp.int32)
-    before = (experts[None, :] < experts[:, None]) | (
-        (experts[None, :] == experts[:, None]) & (position[None, :] < position[:, None])
-    )
-    rank = jnp.sum(before, axis=1, dtype=jnp.int32)
-    placed = rank[None, :] == position[:, None]
-    order = jnp.sum(jnp.where(placed, position[None, :], 0), axis=1, dtype=jnp.int32)
-    sorted_experts = jnp.sum(jnp.where(placed, experts[None, :], 0), axis=1, dtype=jnp.int32)
-    previous = jnp.concatenate([jnp.full((1,), -1, jnp.int32), sorted_experts[:-1]])
-    keep = (sorted_experts == previous).astype(jnp.int32)
-    blocks = jnp.arange(n, dtype=jnp.int32)
-    block_of = jnp.sum(jnp.where(owner[None, :] == blocks[:, None], blocks[None, :], 0), axis=1, dtype=jnp.int32)
-    expert_of = block_of // halves
-    same = experts[None, :] == expert_of[:, None]
-    upto = jnp.sum(experts[None, :] <= expert_of[:, None], axis=1, dtype=jnp.int32)
-    source = jnp.where(jnp.any(same, axis=1), upto - 1, size)
-    wanted = (halves * experts[:, None] + jnp.arange(halves, dtype=jnp.int32)[None, :]).reshape(-1)
-    fetch = jnp.sum(jnp.where(wanted[:, None] == blocks[None, :], owner[None, :], 0), axis=1, dtype=jnp.int32)
-    mine = jnp.sum(jnp.where(blocks == me, expert_of, 0), dtype=jnp.int32)
-    labels = jnp.arange(counts.shape[0], dtype=jnp.int32)
-    count = jnp.sum(jnp.where(labels == mine, counts, 0), dtype=jnp.int32)
-    return jnp.concatenate([order, keep, source, block_of % halves, fetch, count[None]])
 
 
 def on_device(n, partials, counts, slot_expert, owner, left, right, left_root, right_root):
@@ -272,22 +277,24 @@
     chunks = max(1, min(CHUNKS, rows // (16 * size)))
     sub = rows // chunks // size
     full_cols = right.shape[2]
-    table = index_table(n, groups, halves, counts, slot_expert, owner)
     anywhere = pl.BlockSpec(memory_space=pl.ANY)
     bf16 = jnp.bfloat16
     dma = pltpu.SemaphoreType.DMA
-    update, left_next, right_next = pl.pallas_call(
+    scalars = pl.BlockSpec(memory_space=pltpu.SMEM)
+    fixed = pl.BlockSpec(memory_space=pltpu.HBM)
+    return pl.pallas_call(
         functools.partial(kernel, n, groups, chunks),
         out_shape=(
             jax.ShapeDtypeStruct(partials.shape, bf16),
             jax.ShapeDtypeStruct(left.shape, jnp.float32),
             jax.ShapeDtypeStruct(right.shape, jnp.float32),
         ),
-        in_specs=[pl.BlockSpec(memory_space=pltpu.SMEM)] + [anywhere] * 5,
+        in_specs=[scalars] * 3 + [fixed] * 5,
         out_specs=(anywhere,) * 3,
         scratch_shapes=[
+            pltpu.SMEM((size + 2 * n,), jnp.int32),
             [pltpu.VMEM((size, halves, sub, cols), bf16)] * chunks,
-            pltpu.VMEM((size + 1, halves, sub, cols), bf16),
+            pltpu.VMEM((size + 1, halves, sub, cols), jnp.float32),
             pltpu.VMEM((chunks, n, sub, cols), bf16),
             pltpu.VMEM((chunks, n, sub, cols), bf16),
             pltpu.VMEM((rows, full_cols), bf16),
@@ -304,11 +311,9 @@
         + [dma((chunks,))] * 10
         + [dma((2,))],
         compiler_params=pltpu.CompilerParams(
-            collective_id=0, has_side_effects=True, vmem_limit_bytes=48 * 1024 * 1024
+            collective_id=0, has_side_effects=True, vmem_limit_bytes=60 * 1024 * 1024
         ),
-    )(table, partials, left, right, left_root, right_root)
-    return update, left_next, right_next
-
+    )(counts, slot_expert, owner, partials, left, right, left_root, right_root)
 
 def solution(mesh):
     return jax.shard_map(

time: 114 us -> 104 us (0.912)
  other arithmetic: 4.82 us -> 0 us
  local copies, waits for them, and re-layouts: 9.03 us -> 5.9 us
  Pallas kernels: 98.8 us -> 97.6 us
    reduce_sum x6 -> x0, other arithmetic: 3.85 us -> none  [the longest x1 1.94 us: index_table(): count = jnp.sum(jnp.where(labels == mine, counts, 0), dtype=jnp.int32)]
    unnamed x11 -> x7, local copies, waits for them, and re-layouts: 8.22 us -> 5.9 us
    pallas_call x1, Pallas kernels: 98.8 us -> 97.6 us  [on_device(): pl.pallas_call(functools.partial(kernel, n, groups, chunks), out_shape=(j...]
where the time goes in v2:
time: 104 us
  Pallas kernels  97.6 us (94%)
  local copies, waits for them, and re-layouts  5.9 us (6%)
    pallas_call x1, Pallas kernels, on_device(): pl.pallas_call(functools.partial(kernel, n, groups, chunks), out_shape=(j...  97.6 us
    unnamed x7, local copies, waits for them, and re-layouts  5.9 us

profile of v2, /device:TPU:9, one launch (start us, length us, event | category | flops | bytes accessed | tf_op | source)
XLA Modules:
  0.0 104.1 jit_solution(11920637847533686930)
XLA Ops:
  0.6 97.6 %shard_map.103 = (bf16[1,2,1024,384]{3,2,1,0:T(8,128)(2,1)}, f32[1,512,1024]{2,1,0:T(8,128)}, f32[1,384,768]{2,1,0:T(8,128)}) custom-call(s32[8]{0:T(128)} %counts.1, s32[16]{0:T(128)} %slot_expert.1, s32[16]{0:T(128)} %owner.1, bf16[1,2,1024,384]{3,2,1,0:T(8,128)(2,1)} %partials.1, f32[1,512,1024]{2,1,0:T(8,128)} %left.1, f32[1,384,768]{2,1,0:T(8,128)} %right.1, ...), custom_call_target="tpu_custom_call" | custom-call | tf_op jit(solution)/shard_map/pallas_call | solution.py:285
  98.2 0.0 copy-start
  98.2 2.9 %copy.14 = bf16[1,2,1024,384]{3,2,1,0:T(8,128)(2,1)} copy(bf16[1,2,1024,384]{3,2,1,0:T(8,128)(2,1)} %get-tuple-element.6) | data formatting | bytes 3145728
  101.1 0.0 copy-done
  101.1 0.0 copy-start.1
  101.1 1.3 %copy.15 = f32[1,512,1024]{2,1,0:T(8,128)} copy(f32[1,512,1024]{2,1,0:T(8,128)S(1)} %copy-done) | data formatting | bytes 4194304
  102.4 0.7 copy-done.1
  103.1 1.0 copy.16
Async XLA Ops:
  98.2 2.9 %copy-start = (f32[1,512,1024]{2,1,0:T(8,128)S(1)}, f32[1,512,1024]{2,1,0:T(8,128)}, u32[]{:S(2)}) copy-start(f32[1,512,1024]{2,1,0:T(8,128)} %get-tuple-element.7) | copy-start | bytes 6291460
  101.1 2.0 %copy-start.1 = (f32[1,384,768]{2,1,0:T(8,128)S(1)}, f32[1,384,768]{2,1,0:T(8,128)}, u32[]{:S(2)}) copy-start(f32[1,384,768]{2,1,0:T(8,128)} %get-tuple-element.8) | copy-start | bytes 3538948

commit v3 on v2

--- a/solution.py
+++ b/solution.py
@@ -10,6 +10,7 @@
 GROUPS = 2
 CHUNKS = 4
 AHEAD = 3
+PIECES = 2
 
 
 def kernel(
@@ -270,6 +271,29 @@
         wait_bytes(update.at[0, :, pl.ds(chunk * part, part), :], recv_d.at[chunk])
 
 
+def store_kernel(*refs):
+    count = len(refs) // 3
+    sources, targets, buffers = refs[:count], refs[count : 2 * count], refs[2 * count : 3 * count]
+    load_sem, store_sem = refs[3 * count :]
+    loads, stores = [], []
+    for source, target, buffer in zip(sources, targets, buffers):
+        rows = source.shape[-2] // PIECES
+        for lead in range(source.shape[1] if len(source.shape) == 4 else 1):
+            for piece in range(PIECES):
+                at = pl.ds(piece * rows, rows)
+                at = (0, lead, at) if len(source.shape) == 4 else (0, at)
+                index = len(loads)
+                loads.append(pltpu.make_async_copy(source.at[at], buffer.at[at], load_sem.at[index]))
+                stores.append(pltpu.make_async_copy(buffer.at[at], target.at[at], store_sem.at[index]))
+    for load in loads:
+        load.start()
+    for load, store in zip(loads, stores):
+        load.wait()
+        store.start()
+    for store in stores:
+        store.wait()
+
+
 def on_device(n, partials, counts, slot_expert, owner, left, right, left_root, right_root):
     halves, rows, cols = partials.shape[1:]
     groups = GROUPS
@@ -282,7 +306,7 @@
     dma = pltpu.SemaphoreType.DMA
     scalars = pl.BlockSpec(memory_space=pltpu.SMEM)
     fixed = pl.BlockSpec(memory_space=pltpu.HBM)
-    return pl.pallas_call(
+    results = pl.pallas_call(
         functools.partial(kernel, n, groups, chunks),
         out_shape=(
             jax.ShapeDtypeStruct(partials.shape, bf16),
@@ -314,6 +338,16 @@
             collective_id=0, has_side_effects=True, vmem_limit_bytes=60 * 1024 * 1024
         ),
     )(counts, slot_expert, owner, partials, left, right, left_root, right_root)
+    copies = PIECES * (halves + 2)
+    return pl.pallas_call(
+        store_kernel,
+        out_shape=tuple(jax.ShapeDtypeStruct(result.shape, result.dtype) for result in results),
+        in_specs=[anywhere] * 3,
+        out_specs=(anywhere,) * 3,
+        scratch_shapes=[pltpu.VMEM(result.shape, result.dtype) for result in results]
+        + [dma((copies,)), dma((copies,))],
+        compiler_params=pltpu.CompilerParams(vmem_limit_bytes=60 * 1024 * 1024),
+    )(*results)
 
 def solution(mesh):
     return jax.shard_map(

time: 104 us -> 103 us (level)
  local copies, waits for them, and re-layouts: 5.9 us -> 0 us
  Pallas kernels: 97.6 us -> 102 us
    unnamed x7 -> x0, local copies, waits for them, and re-layouts: 5.9 us -> none
    pallas_call x0 -> x1, Pallas kernels: none -> 4.42 us  [on_device(): pl.pallas_call(store_kernel, out_shape=tuple((jax.ShapeDtypeStruct(result...]
where the time goes in v3:
time: 103 us
  Pallas kernels  102 us (99%)
    pallas_call x1, Pallas kernels, on_device(): pl.pallas_call(functools.partial(kernel, n, groups, chunks), out_shape=(j...  97.6 us
    pallas_call x1, Pallas kernels, on_device(): pl.pallas_call(store_kernel, out_shape=tuple((jax.ShapeDtypeStruct(result...  4.42 us

profile of v3, /device:TPU:9, one launch (start us, length us, event | category | flops | bytes accessed | tf_op | source)
XLA Modules:
  0.0 102.6 jit_solution(13219597424262022295)
XLA Ops:
  0.6 97.6 %shard_map.103 = (bf16[1,2,1024,384]{3,2,1,0:T(8,128)(2,1)}, f32[1,512,1024]{2,1,0:T(8,128)}, f32[1,384,768]{2,1,0:T(8,128)}) custom-call(s32[8]{0:T(128)} %counts.1, s32[16]{0:T(128)} %slot_expert.1, s32[16]{0:T(128)} %owner.1, bf16[1,2,1024,384]{3,2,1,0:T(8,128)(2,1)} %partials.1, f32[1,512,1024]{2,1,0:T(8,128)} %left.1, f32[1,384,768]{2,1,0:T(8,128)} %right.1, ...), custom_call_target="tpu_custom_call" | custom-call | tf_op jit(solution)/shard_map/pallas_call | solution.py:309
  98.2 4.4 %shard_map.104 = (bf16[1,2,1024,384]{3,2,1,0:T(8,128)(2,1)}, f32[1,512,1024]{2,1,0:T(8,128)}, f32[1,384,768]{2,1,0:T(8,128)}) custom-call(bf16[1,2,1024,384]{3,2,1,0:T(8,128)(2,1)} %get-tuple-element.6.refs_0_, f32[1,512,1024]{2,1,0:T(8,128)} %get-tuple-element.7.refs_1_, f32[1,384,768]{2,1,0:T(8,128)} %get-tuple-element.8.refs_2_), custom_call_target="tpu_custom_call" | custom-call | tf_op jit(solution)/shard_map/pallas_call | solution.py:342

commit v4 on v3

--- a/solution.py
+++ b/solution.py
@@ -10,7 +10,7 @@
 GROUPS = 2
 CHUNKS = 4
 AHEAD = 3
-PIECES = 2
+PIECES = 1
 
 
 def kernel(
@@ -63,6 +63,9 @@
 
     lax.fori_loop(1, n, greet, 0)
     pl.semaphore_signal(barrier, inc=1, device_id={"mp": 1 - core}, device_id_type=pl.DeviceIdType.MESH)
+    for load in loads:
+        load.start()
+    running[size] = jnp.zeros_like(running[size])
     pl.semaphore_wait(barrier, n)
 
     def scatter_partials(chunk):
@@ -208,9 +211,6 @@
 
     for chunk in range(min(AHEAD, chunks)):
         scatter_partials(chunk)
-    for load in loads:
-        load.start()
-    running[size] = jnp.zeros_like(running[size])
     fill_table()
     loads[0].wait()
     for chunk in range(chunks):

time: 103 us -> 102 us (level)
  no operation moved by 1% of the time
where the time goes in v4:
time: 102 us
  Pallas kernels  102 us (100%)
    pallas_call x1, Pallas kernels, on_device(): pl.pallas_call(functools.partial(kernel, n, groups, chunks), out_shape=(j...  97.5 us
    pallas_call x1, Pallas kernels, on_device(): pl.pallas_call(store_kernel, out_shape=tuple((jax.ShapeDtypeStruct(result...  4.03 us

profile of v4, /device:TPU:9, one launch (start us, length us, event | category | flops | bytes accessed | tf_op | source)
XLA Modules:
  0.0 102.2 jit_solution(17618574465975421813)
XLA Ops:
  0.6 97.5 %shard_map.103 = (bf16[1,2,1024,384]{3,2,1,0:T(8,128)(2,1)}, f32[1,512,1024]{2,1,0:T(8,128)}, f32[1,384,768]{2,1,0:T(8,128)}) custom-call(s32[8]{0:T(128)} %counts.1, s32[16]{0:T(128)} %slot_expert.1, s32[16]{0:T(128)} %owner.1, bf16[1,2,1024,384]{3,2,1,0:T(8,128)(2,1)} %partials.1, f32[1,512,1024]{2,1,0:T(8,128)} %left.1, f32[1,384,768]{2,1,0:T(8,128)} %right.1, ...), custom_call_target="tpu_custom_call" | custom-call | tf_op jit(solution)/shard_map/pallas_call | solution.py:309
  98.2 4.0 %shard_map.104 = (bf16[1,2,1024,384]{3,2,1,0:T(8,128)(2,1)}, f32[1,512,1024]{2,1,0:T(8,128)}, f32[1,384,768]{2,1,0:T(8,128)}) custom-call(bf16[1,2,1024,384]{3,2,1,0:T(8,128)(2,1)} %get-tuple-element.6.refs_0_, f32[1,512,1024]{2,1,0:T(8,128)} %get-tuple-element.7.refs_1_, f32[1,384,768]{2,1,0:T(8,128)} %get-tuple-element.8.refs_2_), custom_call_target="tpu_custom_call" | custom-call | tf_op jit(solution)/shard_map/pallas_call | solution.py:342
